TPU v7x, 1024 devices: a whole 4x8x16 slice. The times are simulated.
1024 devices in a mesh: tok: 64 (over x_hi, z, core), ten: 16 (over y, x_lo).
Axes of the slice: x: 4 (x_hi: 2, x_lo: 2; x = x_hi * 2 + x_lo), y: 8, z: 16, core: 2. Of those that a mesh axis runs over, the one named last changes fastest.
Arguments:
- counts: int32 [4096, 128256], P('ten', 'tok'), may hold values from 0 to 31
- u_factor: float32 [64, 4096], P('tok', 'ten'), may hold values from -2.5 to 2.5
- u_accum: float32 [64, 4096], P('tok', 'ten'), may hold values from 8016 to 513024
- v_factor: float32 [64, 128256], P('ten', 'tok'), may hold values from -2.5 to 2.5
- v_accum: float32 [64, 128256], P('ten', 'tok'), may hold values from 256 to 16384
Outputs:
- u_next: float32 [64, 4096], P('tok', 'ten')
- u_accum_next: float32 [64, 4096], P('tok', 'ten')
- v_next: float32 [64, 128256], P('ten', 'tok')
- v_accum_next: float32 [64, 128256], P('ten', 'tok')
All inputs are finite; a program needn't handle non-finite values.
Results may differ from a plain program's by a relative error of at most 0.0076.
Values may be sent and summed in bfloat16 or wider, within the bound.
A program may use at most 32 MiB of HBM per device.

v0:
```python
import jax
import jax.numpy as jnp
from jax import lax
from jax.sharding import PartitionSpec as P

weight_scale = 0.5
step_rate = 0.3


def residual(low_tile, v_tile, counts):
    logits = lax.dot_general(
        low_tile, v_tile, (((0,), (0,)), ((), ())), preferred_element_type=jnp.float32
    )
    weighted = weight_scale * counts.astype(jnp.float32)
    return (weighted - (1.0 + weighted) * jax.nn.sigmoid(logits)).astype(jnp.bfloat16)


def gather_tenant(low_rows):
    return lax.all_gather(low_rows, "tok", axis=0, tiled=True)


def shards(counts, u_factor, u_accum, v_factor, v_accum):
    v_tile = lax.all_gather(v_factor.astype(jnp.bfloat16), "ten", axis=0, tiled=True)
    u_tile = gather_tenant(u_factor.astype(jnp.bfloat16))
    resid = residual(u_tile, v_tile, counts)
    grad_u = lax.psum_scatter(
        lax.dot_general(
            v_tile, resid, (((1,), (1,)), ((), ())), preferred_element_type=jnp.float32
        ),
        "tok",
        scatter_dimension=0,
        tiled=True,
    )
    u_accum_next = u_accum + grad_u * grad_u
    u_next = u_factor + step_rate * grad_u / jnp.sqrt(u_accum_next)
    u_fresh = gather_tenant(u_next.astype(jnp.bfloat16))
    resid_fresh = residual(u_fresh, v_tile, counts)
    grad_v = lax.psum_scatter(
        jnp.dot(u_fresh, resid_fresh, preferred_element_type=jnp.float32),
        "ten",
        scatter_dimension=0,
        tiled=True,
    )
    v_accum_next = v_accum + grad_v * grad_v
    v_next = v_factor + step_rate * grad_v / jnp.sqrt(v_accum_next)
    return (u_next, u_accum_next, v_next, v_accum_next)


def solution(mesh):
    return jax.shard_map(
        shards,
        mesh=mesh,
        in_specs=(
            P("ten", "tok"),
            P("tok", "ten"),
            P("tok", "ten"),
            P("ten", "tok"),
            P("ten", "tok"),
        ),
        out_specs=(P("tok", "ten"), P("tok", "ten"), P("ten", "tok"), P("ten", "tok")),
        check_vma=False,
    )
```

profile of v0, /device:TPU:1, one launch (start us, length us, event | category | flops | bytes accessed | tf_op | source)
XLA Modules:
  0.0 797.0 jit_solution(4923615531250024269)
XLA Ops:
  7.2 0.0 all-reduce.5.cloned.1.call-start
  7.2 0.7 convert_bitcast_fusion.2
  7.9 0.8 convert_bitcast_fusion
  8.7 91.4 %all-gather = bf16[64,1,256]{2,1,0:T(2,128)(2,1)S(1)} all-gather(bf16[1,1,256]{2,1,0:T(2,128)(2,1)S(1)} %convert_bitcast_fusion.2), channel_id=1, replica_groups=mesh['tok'=64,'ten'=16] {'tok'}, dimensions={0}, use_global_device_ids=true | all-gather | bytes 33280 | tf_op jit(solution)/shard_map/all_gather | solution.py:19
  100.1 27.2 %all-gather.1 = bf16[16,4,2004]{2,1,0:T(4,128)(2,1)S(1)} all-gather(bf16[1,4,2004]{2,1,0:T(4,128)(2,1)S(1)} %convert_bitcast_fusion), channel_id=1, replica_groups=mesh['tok'=64,'ten'=16] {'ten'}, dimensions={0}, use_global_device_ids=true | all-gather | bytes 272544 | tf_op jit(solution)/shard_map/all_gather | solution.py:23
  127.3 0.1 reshape.11
  127.4 0.0 copy-start.2
  127.4 0.0 copy-start.3
  127.4 0.0 copy-start.4
  127.4 3.4 fusion.14
  130.8 0.0 all-reduce.5.cloned.1.call-update
  130.8 0.0 all-reduce.7.cloned.1.call-start
  130.9 1.3 dynamic-slice
  132.2 444.2 %all-reduce.5.cloned.1.call-done = f32[64,256]{1,0:T(8,128)} async-done(((f32[64,256]{1,0:T(8,128)}), f32[64,256]{1,0:T(8,128)}) %all-reduce.5.cloned.1.call-update) | async-done | bytes 65552
  576.3 0.0 copy-done.2
  576.3 0.0 copy-done.3
  576.3 1.9 convert_bitcast_fusion.1
  578.3 75.7 %all-gather.2 = bf16[64,1,256]{2,1,0:T(2,128)(2,1)S(1)} all-gather(bf16[1,1,256]{2,1,0:T(2,128)(2,1)S(1)} %get-tuple-element.6), channel_id=1, replica_groups=mesh['tok'=64,'ten'=16] {'tok'}, dimensions={0}, use_global_device_ids=true | all-gather | bytes 33280 | tf_op jit(solution)/shard_map/all_gather | solution.py:19
  653.9 0.0 copy-done.4
  654.0 1.9 fusion.12
  655.9 0.0 all-reduce.7.cloned.1.call-update
  655.9 1.3 dynamic-slice.2
  657.8 130.8 %all-reduce.7.cloned.1.call-done = f32[64,2004]{1,0:T(8,128)} async-done(((f32[64,2004]{1,0:T(8,128)}), f32[64,2004]{1,0:T(8,128)}) %all-reduce.7.cloned.1.call-update) | async-done | bytes 513040
  788.7 1.5 multiply_add_fusion
  (4 shorter events, 0.0 us)
Async XLA Ops:
  7.2 569.2 %all-reduce.5.cloned.1.call-start = ((), (), s32[]{:S(2)}) async-start(), calls=%async_computation | async-start | bytes 131072
  127.4 448.9 %copy-start.2 = (f32[1,256]{1,0:T(1,128)S(1)}, f32[1,256]{1,0:T(1,128)}, u32[]{:S(2)}) copy-start(f32[1,256]{1,0:T(1,128)} %param.6) | copy-start | bytes 3076
  127.4 448.9 %copy-start.3 = (f32[1,256]{1,0:T(1,128)S(1)}, f32[1,256]{1,0:T(1,128)}, u32[]{:S(2)}) copy-start(f32[1,256]{1,0:T(1,128)} %param.7) | copy-start | bytes 3076
  127.4 526.5 %copy-start.4 = (s32[256,2004]{0,1:T(8,128)S(1)}, s32[256,2004]{0,1:T(8,128)}, u32[]{:S(2)}) copy-start(s32[256,2004]{0,1:T(8,128)} %param.5) | copy-start | bytes 6156292
  130.8 657.8 %all-reduce.7.cloned.1.call-start = ((), (), s32[]{:S(2)}) async-start(), calls=%async_computation.1 | async-start | bytes 1048576
  653.9 134.7 %copy-start = (f32[4,2004]{1,0:T(4,128)S(1)}, f32[4,2004]{1,0:T(4,128)}, u32[]{:S(2)}) copy-start(f32[4,2004]{1,0:T(4,128)} %param.8) | copy-start | bytes 96196
  654.0 134.7 %copy-start.1 = (f32[4,2004]{1,0:T(4,128)S(1)}, f32[4,2004]{1,0:T(4,128)}, u32[]{:S(2)}) copy-start(f32[4,2004]{1,0:T(4,128)} %param.9) | copy-start | bytes 96196
Sparse Core Ops, SparseCore 0:
  130.9 445.3 all-reduce.4
  656.0 132.5 all-reduce.6
where the time goes:
time: 807 us; the launch traced here: 797 us
  waiting for transfers between devices  575 us (71%)
  blocking collectives  194 us (24%)
  between operations  14.7 us (2%)
    unnamed x4, waiting for transfers between devices  575 us
    all_gather x2, blocking collectives, gather_tenant(): return lax.all_gather(low_rows, 'tok', axis=0, tiled=True)  167 us
    all_gather x1, blocking collectives, shards(): lax.all_gather(v_factor.astype(jnp.bfloat16), 'ten', axis=0, tiled=True)  27.2 us
  transfers between devices with their start and end apart: 2, of which 2 were waited for; matrix products, arithmetic and copies ran while one was open for 0% of the time, Pallas kernels for 0%

commit v1 on v0

v1 whole, which is shorter than its diff:
```python
import jax
import jax.numpy as jnp
from jax import lax
from jax.experimental import pallas as pl
from jax.experimental.pallas import tpu as pltpu
from jax.sharding import PartitionSpec as P

MESH = pl.DeviceIdType.MESH
step_rate = 0.3
RANK = 64
TEN_DEV = 256
TOK_DEV = 2004
PAD = 2048
CHUNK = 512
CHUNKS = PAD // CHUNK
f32, bf16 = jnp.float32, jnp.bfloat16


def place():
    tok, ten = lax.axis_index("tok"), lax.axis_index("ten")
    return tok // 32, (tok // 2) % 16, tok % 2, ten // 2, ten % 2


def tok_at(half, z, core):
    return {"tok": half * 32 + z * 2 + core}


def far_first(step, size):
    return size // 2 + ((step + 1) // 2) * (1 - 2 * (step % 2))


def each_z(body):
    _, z, _, _, _ = place()

    def one(step, carry):
        body((z + far_first(step, 16)) % 16)
        return carry

    lax.fori_loop(0, 15, one, 0)


def each_quad(body):
    half, _, core, _, _ = place()
    for dh, dc in ((1, 1), (1, 0), (0, 1)):
        body((half + dh) % 2, (core + dc) % 2)


def each_tok(body):
    half, z, core, _, _ = place()

    def one(step, carry):
        peer_z = (z + far_first(step, 16)) % 16
        for dh, dc in ((1, 1), (1, 0), (0, 1), (0, 0)):
            body((half + dh) % 2, peer_z, (core + dc) % 2)
        return carry

    lax.fori_loop(0, 15, one, 0)
    each_quad(lambda h, c: body(h, z, c))


def each_ten(body):
    _, _, _, y, x = place()

    def one(step, carry):
        peer_y = (y + far_first(step, 8)) % 8
        for dx in (1, 0):
            body(peer_y * 2 + (x + dx) % 2)
        return carry

    lax.fori_loop(0, 7, one, 0)
    body(y * 2 + (x + 1) % 2)


def send(src, dst, sems, phase, peer):
    send_sem, recv_sem = sems
    pltpu.make_async_remote_copy(
        src_ref=src,
        dst_ref=dst,
        send_sem=send_sem.at[phase],
        recv_sem=recv_sem.at[phase],
        device_id=peer,
        device_id_type=MESH,
    ).start()


def wait_bytes(like, sem):
    pltpu.make_async_copy(like, like, sem).wait()


def kernel(
    counts, u_factor, u_accum, v_factor, v_accum,
    u_next, u_accum_next, v_next, v_accum_next,
    cnt, weight, u_in, ua_in, v_in, va_in, v_rows, u_row, ua_row,
    v_all, v_ranks, v_half, order, u_all, ua_all,
    gu_out, gu_in, gu_z, u_rows, fresh, gv_out, gv_in, gv_sum, g_tile,
    local_sem, send_sem, recv_sem,
):
    half, z, core, y, x = place()
    ten = y * 2 + x
    quad = half * 2 + core
    slot = quad * 16 + z
    sems = (send_sem, recv_sem)

    loads = [
        pltpu.make_async_copy(src, dst, local_sem.at[i])
        for i, (src, dst) in enumerate(
            ((v_factor, v_in), (u_factor, u_in), (u_accum, ua_in), (v_accum, va_in))
        )
    ]
    for q in range(CHUNKS):
        rows = pl.ds(q * CHUNK, min(CHUNK, TOK_DEV - q * CHUNK))
        loads.append(pltpu.make_async_copy(counts.at[rows], cnt.at[rows], local_sem.at[4 + q]))
    for load in loads:
        load.start()

    barrier = pltpu.get_barrier_semaphore()

    def greet(peer):
        pl.semaphore_signal(barrier, inc=1, device_id=peer, device_id_type=MESH)

    each_tok(lambda h, pz, c: greet(tok_at(h, pz, c)))
    each_ten(lambda peer: greet({"ten": peer}))

    v_rows[60:64, :] = jnp.zeros((4, 128), f32)
    loads[0].wait()
    for b in range(16):
        width = min(128, TOK_DEV - b * 128)
        v_rows[4 * b : 4 * b + 4, :width] = v_in[:, b * 128 : b * 128 + width]
    v_all[ten] = v_rows[...].astype(bf16)
    loads[1].wait()
    loads[2].wait()
    for b in range(2):
        u_row[b : b + 1, :] = u_in[:, b * 128 : b * 128 + 128]
        ua_row[b : b + 1, :] = ua_in[:, b * 128 : b * 128 + 128]
    u_all[slot] = u_row[...]
    ua_all[z] = ua_row[...]

    pl.semaphore_wait(barrier, 78)

    each_tok(lambda h, pz, c: send(u_row, u_all.at[slot], sems, 0, tok_at(h, pz, c)))
    each_ten(lambda peer: send(v_all.at[ten], v_all.at[ten], sems, 2, {"ten": peer}))
    each_z(lambda pz: send(ua_row, ua_all.at[z], sems, 1, tok_at(half, pz, core)))

    row = lax.broadcasted_iota(jnp.int32, (256, 256), 0)
    col = lax.broadcasted_iota(jnp.int32, (256, 256), 1)
    rank = (row >> 4) * 4 + (row & 3)
    col_rank = (col & 32) + (col & 15) * 2 + ((col >> 4) & 1)
    same = (((row >> 2) & 3) == (col >> 6)) & (rank == col_rank)
    order[...] = jnp.where(same, 1.0, 0.0).astype(bf16)

    weight[PAD - 48 :, :] = jnp.zeros((48, TEN_DEV), bf16)
    for q in range(CHUNKS):
        loads[4 + q].wait()
        rows = slice(q * CHUNK, min(q * CHUNK + CHUNK, TOK_DEV))
        weight[rows, :] = (0.5 + 0.25 * cnt[rows, :].astype(f32)).astype(bf16)

    wait_bytes(v_all.at[pl.ds(0, 15)], recv_sem.at[2])
    for q in range(CHUNKS):
        block = v_all[:, 16 * q : 16 * q + 16, :].reshape(256, 128)
        ranks = lax.dot_general(
            order[...], block, (((0,), (0,)), ((), ())), preferred_element_type=f32
        )
        for b in range(4):
            start = q * CHUNK + b * 128
            v_ranks[:, start : start + 128] = ranks[64 * b : 64 * b + 64, :].astype(bf16)
            v_half[start : start + 128, :] = (0.5 * ranks[64 * b : 64 * b + 64, :]).T.astype(bf16)

    def residual(low, q):
        rows = slice(q * CHUNK, (q + 1) * CHUNK)
        t = jnp.tanh(jnp.dot(v_half[rows, :], low, preferred_element_type=f32))
        return (weight[rows, :].astype(f32) * (1.0 - t) - 1.0).astype(bf16)

    wait_bytes(u_all.at[pl.ds(0, 63)], recv_sem.at[0])
    u_full = jnp.concatenate([u_all[:, 0, :], u_all[:, 1, :]], axis=1)
    low = u_full.astype(bf16)
    grad_u = jnp.zeros((RANK, TEN_DEV), f32)
    for q in range(CHUNKS):
        grad_u += jnp.dot(
            v_ranks[:, q * CHUNK : (q + 1) * CHUNK], residual(low, q), preferred_element_type=f32
        )
    gu_out[...] = grad_u.reshape(4, 16, TEN_DEV)

    each_quad(lambda h, c: send(gu_out.at[h * 2 + c], gu_in.at[quad], sems, 3, tok_at(h, z, c)))
    gu_in[quad] = gu_out[quad]
    wait_bytes(gu_in.at[pl.ds(0, 3)], recv_sem.at[3])
    gu_z[z] = ((gu_in[0] + gu_in[1]) + (gu_in[2] + gu_in[3])).astype(bf16)
    each_z(lambda pz: send(gu_z.at[z], gu_z.at[z], sems, 4, tok_at(half, pz, core)))
    wait_bytes(ua_all.at[pl.ds(0, 15)], recv_sem.at[1])
    mine = u_all[pl.ds(quad * 16, 16)]
    factor = jnp.concatenate([mine[:, 0, :], mine[:, 1, :]], axis=1)
    accum = jnp.concatenate([ua_all[:, 0, :], ua_all[:, 1, :]], axis=1)
    wait_bytes(gu_z.at[pl.ds(0, 15)], recv_sem.at[4])
    grad = jnp.sum(gu_z[...].astype(f32), axis=0)
    accum = accum + grad * grad
    factor = factor + step_rate * grad / jnp.sqrt(accum)
    fresh[quad] = factor.astype(bf16)
    each_quad(lambda h, c: send(fresh.at[quad], fresh.at[quad], sems, 5, tok_at(h, z, c)))
    u_rows[0] = factor
    u_rows[1] = accum
    u_next[...] = u_rows[0, pl.ds(z, 1), :]
    u_accum_next[...] = u_rows[1, pl.ds(z, 1), :]
    wait_bytes(fresh.at[pl.ds(0, 3)], recv_sem.at[5])

    low = fresh[...].reshape(RANK, TEN_DEV)
    for q in range(CHUNKS):
        part = lax.dot_general(
            low, residual(low, q), (((1,), (1,)), ((), ())), preferred_element_type=f32
        ).astype(bf16)
        stacked = jnp.concatenate([part[:, 128 * b : 128 * b + 128] for b in range(4)], axis=0)
        pieces = jnp.dot(order[...], stacked, preferred_element_type=f32).astype(bf16)
        gv_out[q] = pieces.reshape(16, 16, 128)
        each_ten(lambda peer: send(gv_out.at[q, peer], gv_in.at[q, ten], sems, 6 + q, {"ten": peer}))
        gv_in[q, ten] = gv_out[q, ten]

    loads[3].wait()
    for q in range(CHUNKS):
        wait_bytes(gv_in.at[q, pl.ds(0, 15)], recv_sem.at[6 + q])
        gv_sum[...] = jnp.sum(gv_in[q].astype(f32), axis=0)
        for b in range(4):
            start = q * CHUNK + b * 128
            g_tile[:, start : start + 128] = gv_sum[4 * b : 4 * b + 4, :]
    grad = g_tile[:, :TOK_DEV]
    accum = va_in[...] + grad * grad
    v_accum_next[...] = accum
    v_next[...] = v_in[...] + step_rate * grad / jnp.sqrt(accum)

    wait_bytes(u_all.at[pl.ds(0, 63)], send_sem.at[0])
    wait_bytes(ua_all.at[pl.ds(0, 15)], send_sem.at[1])
    wait_bytes(v_all.at[pl.ds(0, 15)], send_sem.at[2])
    wait_bytes(gu_in.at[pl.ds(0, 3)], send_sem.at[3])
    wait_bytes(gu_z.at[pl.ds(0, 15)], send_sem.at[4])
    wait_bytes(fresh.at[pl.ds(0, 3)], send_sem.at[5])
    for q in range(CHUNKS):
        wait_bytes(gv_in.at[q, pl.ds(0, 15)], send_sem.at[6 + q])


def store(*refs):
    copies = [
        pltpu.make_async_copy(src, dst, refs[8].at[i])
        for i, (src, dst) in enumerate(zip(refs[:4], refs[4:8]))
    ]
    for copy in copies:
        copy.start()
    for copy in copies:
        copy.wait()


def shards(counts, u_factor, u_accum, v_factor, v_accum):
    vmem = pltpu.VMEM
    results = (
        pl.pallas_call(
            kernel,
            out_shape=tuple(
                jax.ShapeDtypeStruct(like.shape, f32) for like in (u_factor, u_accum, v_factor, v_accum)
            ),
            in_specs=[pl.BlockSpec(memory_space=pl.ANY)] * 5,
            out_specs=(pl.BlockSpec(memory_space=vmem),) * 4,
            scratch_shapes=[
                vmem((TOK_DEV, TEN_DEV), jnp.int32),
                vmem((PAD, TEN_DEV), bf16),
                vmem((1, TEN_DEV), f32),
                vmem((1, TEN_DEV), f32),
                vmem((4, TOK_DEV), f32),
                vmem((4, TOK_DEV), f32),
                vmem((64, 128), f32),
                vmem((2, 128), f32),
                vmem((2, 128), f32),
                vmem((16, 64, 128), bf16),
                vmem((RANK, PAD), bf16),
                vmem((PAD, RANK), bf16),
                vmem((256, 256), bf16),
                vmem((64, 2, 128), f32),
                vmem((16, 2, 128), f32),
                vmem((4, 16, TEN_DEV), f32),
                vmem((4, 16, TEN_DEV), f32),
                vmem((16, 16, TEN_DEV), bf16),
                vmem((2, 16, TEN_DEV), f32),
                vmem((4, 16, TEN_DEV), bf16),
                vmem((CHUNKS, 16, 16, 128), bf16),
                vmem((CHUNKS, 16, 16, 128), bf16),
                vmem((16, 128), f32),
                vmem((4, PAD), f32),
                pltpu.SemaphoreType.DMA((4 + CHUNKS,)),
                pltpu.SemaphoreType.DMA((6 + CHUNKS,)),
                pltpu.SemaphoreType.DMA((6 + CHUNKS,)),
            ],
            compiler_params=pltpu.CompilerParams(
                collective_id=0, has_side_effects=True, vmem_limit_bytes=57 << 20
            ),
        )(counts.T, u_factor, u_accum, v_factor, v_accum)
    )
    return pl.pallas_call(
        store,
        out_shape=tuple(jax.ShapeDtypeStruct(like.shape, f32) for like in results),
        in_specs=[pl.BlockSpec(memory_space=vmem)] * 4,
        out_specs=(pl.BlockSpec(memory_space=pl.ANY),) * 4,
        scratch_shapes=[pltpu.SemaphoreType.DMA((4,))],
    )(*results)


def solution(mesh):
    return jax.shard_map(
        shards,
        mesh=mesh,
        in_specs=(
            P("ten", "tok"),
            P("tok", "ten"),
            P("tok", "ten"),
            P("ten", "tok"),
            P("ten", "tok"),
        ),
        out_specs=(P("tok", "ten"), P("tok", "ten"), P("ten", "tok"), P("ten", "tok")),
        check_vma=False,
    )
```

time: 807 us -> 63.7 us (0.08); the launches traced: 797 us -> 63.5 us
  waiting for transfers between devices: 575 us -> 0 us
  blocking collectives: 194 us -> 0 us
  Pallas kernels: 0 us -> 62.9 us
  between operations: 14.7 us -> 0.64 us
    unnamed x4 -> x0, waiting for transfers between devices: 575 us -> none
    all_gather x3 -> x0, blocking collectives: 194 us -> none  [the longest x2 167 us: gather_tenant(): return lax.all_gather(low_rows, 'tok', axis=0, tiled=True)]
    pallas_call x0 -> x2, Pallas kernels: none -> 62.9 us  [the longest x1 61.4 us: shards(): pl.pallas_call(kernel, out_shape=tuple((jax.ShapeDtypeStruct(like.shape,...]
  transfers between devices with their start and end apart: 2 -> 0, of which waited for: 2 -> 0; matrix products, arithmetic and copies ran while one was open for 0% -> 0% of each run, Pallas kernels for 0% -> 0%
where the time goes in v1:
time: 63.7 us; the launch traced here: 63.5 us
  Pallas kernels  62.9 us (99%)
  between operations  0.64 us (1%)
    pallas_call x1, Pallas kernels, shards(): pl.pallas_call(kernel, out_shape=tuple((jax.ShapeDtypeStruct(like.shape,...  61.4 us
    pallas_call x1, Pallas kernels, shards(): pl.pallas_call(store, out_shape=tuple((jax.ShapeDtypeStruct(like.shape, f...  1.45 us

profile of v1, /device:TPU:1, one launch (start us, length us, event | category | flops | bytes accessed | tf_op | source)
XLA Modules:
  0.0 63.5 jit_solution(5005680860032407687)
XLA Ops:
  0.6 61.4 %shard_map.84 = (f32[1,256]{1,0:T(1,128)}, f32[1,256]{1,0:T(1,128)}, f32[4,2004]{1,0:T(4,128)}, f32[4,2004]{1,0:T(4,128)}) custom-call(s32[2004,256]{1,0:T(8,128)} %bitcast.1, f32[1,256]{1,0:T(1,128)} %u_factor.1, f32[1,256]{1,0:T(1,128)} %u_accum.1, f32[4,2004]{1,0:T(4,128)} %v_factor.1, f32[4,2004]{1,0:T(4,128)} %v_accum.1), custom_call_target="tpu_custom_call" | custom-call | tf_op jit(solution)/shard_map/pallas_call | solution.py:251
  62.1 1.5 %shard_map.85 = (f32[1,256]{1,0:T(1,128)}, f32[1,256]{1,0:T(1,128)}, f32[4,2004]{1,0:T(4,128)}, f32[4,2004]{1,0:T(4,128)}) custom-call(f32[1,256]{1,0:T(1,128)} %get-tuple-element.8.refs_0_, f32[1,256]{1,0:T(1,128)} %get-tuple-element.9.refs_1_, f32[4,2004]{1,0:T(4,128)} %get-tuple-element.10.refs_2_, f32[4,2004]{1,0:T(4,128)} %get-tuple-element.11.refs_3_), custom_call_target="tpu_custom_call" | custom-call | tf_op jit(solution)/shard_map/pallas_call | solution.py:292

commit v2 on v1

--- a/solution.py
+++ b/solution.py
@@ -25,6 +25,10 @@
     return {"tok": half * 32 + z * 2 + core}
 
 
+def ten_at(y, x):
+    return {"ten": y * 2 + x}
+
+
 def far_first(step, size):
     return size // 2 + ((step + 1) // 2) * (1 - 2 * (step % 2))
 
@@ -45,13 +49,25 @@
         body((half + dh) % 2, (core + dc) % 2)
 
 
+def each_core(step, body):
+    half, z, core, _, _ = place()
+    peer_z = (z + far_first(step, 16)) % 16
+    for dh, dc in ((1, 1), (1, 0), (0, 1), (0, 0)):
+        body((half + dh) % 2, peer_z, (core + dc) % 2)
+
+
+def each_x(step, body):
+    _, _, _, y, x = place()
+    peer_y = (y + far_first(step, 8)) % 8
+    for dx in (1, 0):
+        body(peer_y, (x + dx) % 2)
+
+
 def each_tok(body):
-    half, z, core, _, _ = place()
+    _, z, _, _, _ = place()
 
     def one(step, carry):
-        peer_z = (z + far_first(step, 16)) % 16
-        for dh, dc in ((1, 1), (1, 0), (0, 1), (0, 0)):
-            body((half + dh) % 2, peer_z, (core + dc) % 2)
+        each_core(step, body)
         return carry
 
     lax.fori_loop(0, 15, one, 0)
@@ -62,13 +78,21 @@
     _, _, _, y, x = place()
 
     def one(step, carry):
-        peer_y = (y + far_first(step, 8)) % 8
-        for dx in (1, 0):
-            body(peer_y * 2 + (x + dx) % 2)
+        each_x(step, body)
         return carry
 
     lax.fori_loop(0, 7, one, 0)
-    body(y * 2 + (x + 1) % 2)
+    body(y, (x + 1) % 2)
+
+
+def each_y(body):
+    _, _, _, y, _ = place()
+
+    def one(step, carry):
+        body((y + far_first(step, 8)) % 8)
+        return carry
+
+    lax.fori_loop(0, 7, one, 0)
 
 
 def send(src, dst, sems, phase, peer):
@@ -92,11 +116,11 @@
     u_next, u_accum_next, v_next, v_accum_next,
     cnt, weight, u_in, ua_in, v_in, va_in, v_rows, u_row, ua_row,
     v_all, v_ranks, v_half, order, u_all, ua_all,
-    gu_out, gu_in, gu_z, u_rows, fresh, gv_out, gv_in, gv_sum, g_tile,
+    gu_out, gu_in, gu_z, u_rows, fresh, gv_out, gv_in, gv_x, gv_mid, gv_y, gv_sum, g_tile,
     local_sem, send_sem, recv_sem,
 ):
     half, z, core, y, x = place()
-    ten = y * 2 + x
+    ten = x * 8 + y
     quad = half * 2 + core
     slot = quad * 16 + z
     sems = (send_sem, recv_sem)
@@ -119,7 +143,7 @@
         pl.semaphore_signal(barrier, inc=1, device_id=peer, device_id_type=MESH)
 
     each_tok(lambda h, pz, c: greet(tok_at(h, pz, c)))
-    each_ten(lambda peer: greet({"ten": peer}))
+    each_ten(lambda py, px: greet(ten_at(py, px)))
 
     v_rows[60:64, :] = jnp.zeros((4, 128), f32)
     loads[0].wait()
@@ -137,13 +161,30 @@
 
     pl.semaphore_wait(barrier, 78)
 
-    each_tok(lambda h, pz, c: send(u_row, u_all.at[slot], sems, 0, tok_at(h, pz, c)))
-    each_ten(lambda peer: send(v_all.at[ten], v_all.at[ten], sems, 2, {"ten": peer}))
+    def send_u(h, pz, c):
+        send(u_row, u_all.at[slot], sems, 0, tok_at(h, pz, c))
+
+    def send_v(py, px):
+        send(v_all.at[ten], v_all.at[ten], sems, 2, ten_at(py, px))
+
+    def send_both(step, carry):
+        each_core(step, send_u)
+        each_x(step, send_v)
+        return carry
+
+    def send_rest(step, carry):
+        each_core(step, send_u)
+        return carry
+
+    lax.fori_loop(0, 7, send_both, 0)
+    send_v(y, (x + 1) % 2)
+    lax.fori_loop(7, 15, send_rest, 0)
+    each_quad(lambda h, c: send_u(h, z, c))
     each_z(lambda pz: send(ua_row, ua_all.at[z], sems, 1, tok_at(half, pz, core)))
 
     row = lax.broadcasted_iota(jnp.int32, (256, 256), 0)
     col = lax.broadcasted_iota(jnp.int32, (256, 256), 1)
-    rank = (row >> 4) * 4 + (row & 3)
+    rank = ((row >> 4) & 7) * 8 + (row >> 7) * 4 + (row & 3)
     col_rank = (col & 32) + (col & 15) * 2 + ((col >> 4) & 1)
     same = (((row >> 2) & 3) == (col >> 6)) & (rank == col_rank)
     order[...] = jnp.where(same, 1.0, 0.0).astype(bf16)
@@ -209,13 +250,29 @@
         stacked = jnp.concatenate([part[:, 128 * b : 128 * b + 128] for b in range(4)], axis=0)
         pieces = jnp.dot(order[...], stacked, preferred_element_type=f32).astype(bf16)
         gv_out[q] = pieces.reshape(16, 16, 128)
-        each_ten(lambda peer: send(gv_out.at[q, peer], gv_in.at[q, ten], sems, 6 + q, {"ten": peer}))
-        gv_in[q, ten] = gv_out[q, ten]
+        if q % 2 == 0:
+            other = gv_out.at[q, pl.ds((1 - x) * 8, 8)]
+            send(other, gv_x.at[q // 2], sems, 6 + q, ten_at(y, 1 - x))
+        else:
+            each_ten(lambda py, px: send(gv_out.at[q, px * 8 + py], gv_in.at[q // 2, ten], sems, 6 + q, ten_at(py, px)))
+            gv_in[q // 2, ten] = gv_out[q, ten]
+    for q in range(0, CHUNKS, 2):
+        i = q // 2
+        wait_bytes(gv_x.at[i], recv_sem.at[6 + q])
+        pair = gv_out[q, pl.ds(x * 8, 8)].astype(f32) + gv_x[i].astype(f32)
+        gv_mid[i] = pair.astype(bf16)
+        each_y(lambda py: send(gv_mid.at[i, py], gv_y.at[i, y], sems, 6 + CHUNKS + i, ten_at(py, x)))
+        gv_y[i, y] = gv_mid[i, y]
 
     loads[3].wait()
-    for q in range(CHUNKS):
-        wait_bytes(gv_in.at[q, pl.ds(0, 15)], recv_sem.at[6 + q])
-        gv_sum[...] = jnp.sum(gv_in[q].astype(f32), axis=0)
+    for q in (1, 3, 0, 2):
+        i = q // 2
+        if q % 2 == 0:
+            wait_bytes(gv_y.at[i, pl.ds(0, 7)], recv_sem.at[6 + CHUNKS + i])
+            gv_sum[...] = jnp.sum(gv_y[i].astype(f32), axis=0)
+        else:
+            wait_bytes(gv_in.at[i, pl.ds(0, 15)], recv_sem.at[6 + q])
+            gv_sum[...] = jnp.sum(gv_in[i].astype(f32), axis=0)
         for b in range(4):
             start = q * CHUNK + b * 128
             g_tile[:, start : start + 128] = gv_sum[4 * b : 4 * b + 4, :]
@@ -230,8 +287,10 @@
     wait_bytes(gu_in.at[pl.ds(0, 3)], send_sem.at[3])
     wait_bytes(gu_z.at[pl.ds(0, 15)], send_sem.at[4])
     wait_bytes(fresh.at[pl.ds(0, 3)], send_sem.at[5])
-    for q in range(CHUNKS):
-        wait_bytes(gv_in.at[q, pl.ds(0, 15)], send_sem.at[6 + q])
+    for i in range(CHUNKS // 2):
+        wait_bytes(gv_x.at[i], send_sem.at[6 + 2 * i])
+        wait_bytes(gv_in.at[i, pl.ds(0, 15)], send_sem.at[7 + 2 * i])
+        wait_bytes(gv_y.at[i, pl.ds(0, 7)], send_sem.at[6 + CHUNKS + i])
 
 
 def store(*refs):
@@ -277,17 +336,20 @@
                 vmem((2, 16, TEN_DEV), f32),
                 vmem((4, 16, TEN_DEV), bf16),
                 vmem((CHUNKS, 16, 16, 128), bf16),
-                vmem((CHUNKS, 16, 16, 128), bf16),
+                vmem((CHUNKS // 2, 16, 16, 128), bf16),
+                vmem((CHUNKS // 2, 8, 16, 128), bf16),
+                vmem((CHUNKS // 2, 8, 16, 128), bf16),
+                vmem((CHUNKS // 2, 8, 16, 128), bf16),
                 vmem((16, 128), f32),
                 vmem((4, PAD), f32),
                 pltpu.SemaphoreType.DMA((4 + CHUNKS,)),
-                pltpu.SemaphoreType.DMA((6 + CHUNKS,)),
-                pltpu.SemaphoreType.DMA((6 + CHUNKS,)),
+                pltpu.SemaphoreType.DMA((6 + CHUNKS + CHUNKS // 2,)),
+                pltpu.SemaphoreType.DMA((6 + CHUNKS + CHUNKS // 2,)),
             ],
             compiler_params=pltpu.CompilerParams(
-                collective_id=0, has_side_effects=True, vmem_limit_bytes=57 << 20
+                collective_id=0, has_side_effects=True, vmem_limit_bytes=40 << 20
             ),
-        )(counts.T, u_factor, u_accum, v_factor, v_accum)
+        )(*(pltpu.with_memory_space_constraint(a, pltpu.HBM) for a in (counts.T, u_factor, u_accum, v_factor, v_accum)))
     )
     return pl.pallas_call(
         store,
@@ -295,6 +357,7 @@
         in_specs=[pl.BlockSpec(memory_space=vmem)] * 4,
         out_specs=(pl.BlockSpec(memory_space=pl.ANY),) * 4,
         scratch_shapes=[pltpu.SemaphoreType.DMA((4,))],
+        compiler_params=pltpu.CompilerParams(vmem_limit_bytes=1 << 20),
     )(*results)
 
 

time: 63.7 us -> 61.8 us (0.970)
  Pallas kernels: 62.9 us -> 61 us
    pallas_call x1, Pallas kernels: 61.4 us -> 60.3 us  [shards(): pl.pallas_call(kernel, out_shape=tuple((jax.ShapeDtypeStruct(like.shape,...]
    pallas_call x1, Pallas kernels: 1.45 us -> 0.67 us  [shards(): pl.pallas_call(store, out_shape=tuple((jax.ShapeDtypeStruct(like.shape, f...]
where the time goes in v2:
time: 61.8 us; the launch traced here: 61.6 us
  Pallas kernels  61 us (99%)
  between operations  0.64 us (1%)
    pallas_call x1, Pallas kernels, shards(): pl.pallas_call(kernel, out_shape=tuple((jax.ShapeDtypeStruct(like.shape,...  60.3 us

profile of v2, /device:TPU:1, one launch (start us, length us, event | category | flops | bytes accessed | tf_op | source)
XLA Modules:
  0.0 61.6 jit_solution(16054157380464821311)
XLA Ops:
  0.6 60.3 %shard_map.84 = (f32[1,256]{1,0:T(1,128)S(1)}, f32[1,256]{1,0:T(1,128)S(1)}, f32[4,2004]{1,0:T(4,128)S(1)}, f32[4,2004]{1,0:T(4,128)S(1)}) custom-call(s32[2004,256]{1,0:T(8,128)} %bitcast.1, f32[1,256]{1,0:T(1,128)} %u_factor.1, f32[1,256]{1,0:T(1,128)} %u_accum.1, f32[4,2004]{1,0:T(4,128)} %v_factor.1, f32[4,2004]{1,0:T(4,128)} %v_accum.1), custom_call_target="tpu_custom_call" | custom-call | tf_op jit(solution)/shard_map/pallas_call | solution.py:310
  61.0 0.7 %shard_map.85 = (f32[1,256]{1,0:T(1,128)}, f32[1,256]{1,0:T(1,128)}, f32[4,2004]{1,0:T(4,128)}, f32[4,2004]{1,0:T(4,128)}) custom-call(f32[1,256]{1,0:T(1,128)S(1)} %get-tuple-element.8.refs_0_, f32[1,256]{1,0:T(1,128)S(1)} %get-tuple-element.9.refs_1_, f32[4,2004]{1,0:T(4,128)S(1)} %get-tuple-element.10.refs_2_, f32[4,2004]{1,0:T(4,128)S(1)} %get-tuple-element.11.refs_3_), custom_call_target="tpu_custom_call" | custom-call | tf_op jit(solution)/shard_map/pallas_call | solution.py:354

commit v3 on v2

--- a/solution.py
+++ b/solution.py
@@ -13,6 +13,8 @@
 PAD = 2048
 CHUNK = 512
 CHUNKS = PAD // CHUNK
+PAIRED = (0, 1)
+STRAIGHT = tuple(q for q in range(CHUNKS) if q not in PAIRED)
 f32, bf16 = jnp.float32, jnp.bfloat16
 
 
@@ -70,7 +72,7 @@
         each_core(step, body)
         return carry
 
-    lax.fori_loop(0, 15, one, 0)
+    lax.fori_loop(0, 15, one, 0, unroll=5)
     each_quad(lambda h, c: body(h, z, c))
 
 
@@ -81,7 +83,7 @@
         each_x(step, body)
         return carry
 
-    lax.fori_loop(0, 7, one, 0)
+    lax.fori_loop(0, 7, one, 0, unroll=7)
     body(y, (x + 1) % 2)
 
 
@@ -116,13 +118,12 @@
     u_next, u_accum_next, v_next, v_accum_next,
     cnt, weight, u_in, ua_in, v_in, va_in, v_rows, u_row, ua_row,
     v_all, v_ranks, v_half, order, u_all, ua_all,
-    gu_out, gu_in, gu_z, u_rows, fresh, gv_out, gv_in, gv_x, gv_mid, gv_y, gv_sum, g_tile,
+    gu_out, gu_in, gu_z, u_rows, u_pair, u_got, fresh, gv_out, gv_in, gv_x, gv_mid, gv_y, gv_sum, g_tile,
     local_sem, send_sem, recv_sem,
 ):
     half, z, core, y, x = place()
     ten = x * 8 + y
-    quad = half * 2 + core
-    slot = quad * 16 + z
+    slot = half * 32 + core * 16 + z
     sems = (send_sem, recv_sem)
 
     loads = [
@@ -157,7 +158,10 @@
         u_row[b : b + 1, :] = u_in[:, b * 128 : b * 128 + 128]
         ua_row[b : b + 1, :] = ua_in[:, b * 128 : b * 128 + 128]
     u_all[slot] = u_row[...]
-    ua_all[z] = ua_row[...]
+
+    @pl.when(core == 1)
+    def _():
+        ua_all[16 + z] = ua_row[...]
 
     pl.semaphore_wait(barrier, 78)
 
@@ -180,7 +184,12 @@
     send_v(y, (x + 1) % 2)
     lax.fori_loop(7, 15, send_rest, 0)
     each_quad(lambda h, c: send_u(h, z, c))
-    each_z(lambda pz: send(ua_row, ua_all.at[z], sems, 1, tok_at(half, pz, core)))
+    each_z(lambda pz: send(ua_row, ua_all.at[core * 16 + z], sems, 1, tok_at(half, pz, 1)))
+
+    @pl.when(core == 0)
+    def _():
+        send(ua_row, ua_all.at[z], sems, 1, tok_at(half, z, 1))
+
 
     row = lax.broadcasted_iota(jnp.int32, (256, 256), 0)
     col = lax.broadcasted_iota(jnp.int32, (256, 256), 1)
@@ -219,28 +228,43 @@
         grad_u += jnp.dot(
             v_ranks[:, q * CHUNK : (q + 1) * CHUNK], residual(low, q), preferred_element_type=f32
         )
-    gu_out[...] = grad_u.reshape(4, 16, TEN_DEV)
-
-    each_quad(lambda h, c: send(gu_out.at[h * 2 + c], gu_in.at[quad], sems, 3, tok_at(h, z, c)))
-    gu_in[quad] = gu_out[quad]
-    wait_bytes(gu_in.at[pl.ds(0, 3)], recv_sem.at[3])
-    gu_z[z] = ((gu_in[0] + gu_in[1]) + (gu_in[2] + gu_in[3])).astype(bf16)
-    each_z(lambda pz: send(gu_z.at[z], gu_z.at[z], sems, 4, tok_at(half, pz, core)))
-    wait_bytes(ua_all.at[pl.ds(0, 15)], recv_sem.at[1])
-    mine = u_all[pl.ds(quad * 16, 16)]
-    factor = jnp.concatenate([mine[:, 0, :], mine[:, 1, :]], axis=1)
-    accum = jnp.concatenate([ua_all[:, 0, :], ua_all[:, 1, :]], axis=1)
-    wait_bytes(gu_z.at[pl.ds(0, 15)], recv_sem.at[4])
-    grad = jnp.sum(gu_z[...].astype(f32), axis=0)
-    accum = accum + grad * grad
-    factor = factor + step_rate * grad / jnp.sqrt(accum)
-    fresh[quad] = factor.astype(bf16)
-    each_quad(lambda h, c: send(fresh.at[quad], fresh.at[quad], sems, 5, tok_at(h, z, c)))
-    u_rows[0] = factor
-    u_rows[1] = accum
-    u_next[...] = u_rows[0, pl.ds(z, 1), :]
-    u_accum_next[...] = u_rows[1, pl.ds(z, 1), :]
-    wait_bytes(fresh.at[pl.ds(0, 3)], recv_sem.at[5])
+    gu_out[...] = grad_u.reshape(2, 32, TEN_DEV).astype(bf16)
+
+    send(gu_out.at[1 - half], gu_in.at[2 - core], sems, 3, tok_at(1 - half, z, 1))
+
+    @pl.when(core == 0)
+    def _():
+        send(gu_out.at[half], gu_in.at[0], sems, 3, tok_at(half, z, 1))
+
+    @pl.when(core == 1)
+    def _():
+        mine = u_all[pl.ds(half * 32, 32)]
+        wait_bytes(ua_all.at[pl.ds(0, 31)], recv_sem.at[1])
+        factor = jnp.concatenate([mine[:, 0, :], mine[:, 1, :]], axis=1)
+        accum = jnp.concatenate([ua_all[:, 0, :], ua_all[:, 1, :]], axis=1)
+        wait_bytes(gu_in, recv_sem.at[3])
+        total = gu_out[half].astype(f32) + jnp.sum(gu_in[...].astype(f32), axis=0)
+        gu_z[z] = total.astype(bf16)
+        each_z(lambda pz: send(gu_z.at[z], gu_z.at[z], sems, 4, tok_at(half, pz, 1)))
+        wait_bytes(gu_z.at[pl.ds(0, 15)], recv_sem.at[4])
+        grad = jnp.sum(gu_z[...].astype(f32), axis=0)
+        accum = accum + grad * grad
+        factor = factor + step_rate * grad / jnp.sqrt(accum)
+        fresh[half] = factor.astype(bf16)
+        for h, c in ((1 - half, 0), (1 - half, 1), (half, 0)):
+            send(fresh.at[half], fresh.at[half], sems, 5, tok_at(h, z, c))
+        u_rows[0] = factor
+        u_rows[1] = accum
+        for i in range(2):
+            u_pair[i : i + 1, :] = u_rows[i, pl.ds(z, 1), :]
+        send(u_pair, u_got, sems, 6, tok_at(half, z, 0))
+        u_next[...] = u_rows[0, pl.ds(16 + z, 1), :]
+        u_accum_next[...] = u_rows[1, pl.ds(16 + z, 1), :]
+        wait_bytes(fresh.at[0], recv_sem.at[5])
+
+    @pl.when(core == 0)
+    def _():
+        wait_bytes(fresh, recv_sem.at[5])
 
     low = fresh[...].reshape(RANK, TEN_DEV)
     for q in range(CHUNKS):
@@ -250,47 +274,63 @@
         stacked = jnp.concatenate([part[:, 128 * b : 128 * b + 128] for b in range(4)], axis=0)
         pieces = jnp.dot(order[...], stacked, preferred_element_type=f32).astype(bf16)
         gv_out[q] = pieces.reshape(16, 16, 128)
-        if q % 2 == 0:
+        if q in PAIRED:
             other = gv_out.at[q, pl.ds((1 - x) * 8, 8)]
-            send(other, gv_x.at[q // 2], sems, 6 + q, ten_at(y, 1 - x))
+            send(other, gv_x.at[PAIRED.index(q)], sems, 7 + q, ten_at(y, 1 - x))
         else:
-            each_ten(lambda py, px: send(gv_out.at[q, px * 8 + py], gv_in.at[q // 2, ten], sems, 6 + q, ten_at(py, px)))
-            gv_in[q // 2, ten] = gv_out[q, ten]
-    for q in range(0, CHUNKS, 2):
-        i = q // 2
-        wait_bytes(gv_x.at[i], recv_sem.at[6 + q])
+            i = STRAIGHT.index(q)
+            each_ten(lambda py, px: send(gv_out.at[q, px * 8 + py], gv_in.at[i, ten], sems, 7 + q, ten_at(py, px)))
+            gv_in[i, ten] = gv_out[q, ten]
+    for i, q in enumerate(PAIRED):
+        wait_bytes(gv_x.at[i], recv_sem.at[7 + q])
         pair = gv_out[q, pl.ds(x * 8, 8)].astype(f32) + gv_x[i].astype(f32)
         gv_mid[i] = pair.astype(bf16)
-        each_y(lambda py: send(gv_mid.at[i, py], gv_y.at[i, y], sems, 6 + CHUNKS + i, ten_at(py, x)))
+        each_y(lambda py: send(gv_mid.at[i, py], gv_y.at[i, y], sems, 7 + CHUNKS + i, ten_at(py, x)))
         gv_y[i, y] = gv_mid[i, y]
 
     loads[3].wait()
-    for q in (1, 3, 0, 2):
-        i = q // 2
-        if q % 2 == 0:
-            wait_bytes(gv_y.at[i, pl.ds(0, 7)], recv_sem.at[6 + CHUNKS + i])
+    for q in STRAIGHT + PAIRED:
+        if q in PAIRED:
+            i = PAIRED.index(q)
+            wait_bytes(gv_y.at[i, pl.ds(0, 7)], recv_sem.at[7 + CHUNKS + i])
             gv_sum[...] = jnp.sum(gv_y[i].astype(f32), axis=0)
         else:
-            wait_bytes(gv_in.at[i, pl.ds(0, 15)], recv_sem.at[6 + q])
+            i = STRAIGHT.index(q)
+            wait_bytes(gv_in.at[i, pl.ds(0, 15)], recv_sem.at[7 + q])
             gv_sum[...] = jnp.sum(gv_in[i].astype(f32), axis=0)
         for b in range(4):
             start = q * CHUNK + b * 128
             g_tile[:, start : start + 128] = gv_sum[4 * b : 4 * b + 4, :]
-    grad = g_tile[:, :TOK_DEV]
-    accum = va_in[...] + grad * grad
-    v_accum_next[...] = accum
-    v_next[...] = v_in[...] + step_rate * grad / jnp.sqrt(accum)
+        cols = slice(q * CHUNK, min(q * CHUNK + CHUNK, TOK_DEV))
+        grad = g_tile[:, cols]
+        accum = va_in[:, cols] + grad * grad
+        v_accum_next[:, cols] = accum
+        v_next[:, cols] = v_in[:, cols] + step_rate * grad / jnp.sqrt(accum)
 
     wait_bytes(u_all.at[pl.ds(0, 63)], send_sem.at[0])
     wait_bytes(ua_all.at[pl.ds(0, 15)], send_sem.at[1])
     wait_bytes(v_all.at[pl.ds(0, 15)], send_sem.at[2])
-    wait_bytes(gu_in.at[pl.ds(0, 3)], send_sem.at[3])
-    wait_bytes(gu_z.at[pl.ds(0, 15)], send_sem.at[4])
-    wait_bytes(fresh.at[pl.ds(0, 3)], send_sem.at[5])
-    for i in range(CHUNKS // 2):
-        wait_bytes(gv_x.at[i], send_sem.at[6 + 2 * i])
-        wait_bytes(gv_in.at[i, pl.ds(0, 15)], send_sem.at[7 + 2 * i])
-        wait_bytes(gv_y.at[i, pl.ds(0, 7)], send_sem.at[6 + CHUNKS + i])
+    wait_bytes(gu_out.at[0], send_sem.at[3])
+
+    @pl.when(core == 0)
+    def _():
+        wait_bytes(ua_row, send_sem.at[1])
+        wait_bytes(gu_out.at[0], send_sem.at[3])
+        wait_bytes(u_got, recv_sem.at[6])
+        u_next[...] = u_got[0:1, :]
+        u_accum_next[...] = u_got[1:2, :]
+
+    @pl.when(core == 1)
+    def _():
+        wait_bytes(gu_z.at[pl.ds(0, 15)], send_sem.at[4])
+        wait_bytes(gu_in, send_sem.at[5])
+        wait_bytes(u_pair, send_sem.at[6])
+
+    for i, q in enumerate(PAIRED):
+        wait_bytes(gv_x.at[i], send_sem.at[7 + q])
+        wait_bytes(gv_y.at[i, pl.ds(0, 7)], send_sem.at[7 + CHUNKS + i])
+    for i, q in enumerate(STRAIGHT):
+        wait_bytes(gv_in.at[i, pl.ds(0, 15)], send_sem.at[7 + q])
 
 
 def store(*refs):
@@ -329,22 +369,24 @@
                 vmem((PAD, RANK), bf16),
                 vmem((256, 256), bf16),
                 vmem((64, 2, 128), f32),
-                vmem((16, 2, 128), f32),
-                vmem((4, 16, TEN_DEV), f32),
-                vmem((4, 16, TEN_DEV), f32),
-                vmem((16, 16, TEN_DEV), bf16),
-                vmem((2, 16, TEN_DEV), f32),
-                vmem((4, 16, TEN_DEV), bf16),
+                vmem((32, 2, 128), f32),
+                vmem((2, 32, TEN_DEV), bf16),
+                vmem((3, 32, TEN_DEV), bf16),
+                vmem((16, 32, TEN_DEV), bf16),
+                vmem((2, 32, TEN_DEV), f32),
+                vmem((2, TEN_DEV), f32),
+                vmem((2, TEN_DEV), f32),
+                vmem((2, 32, TEN_DEV), bf16),
                 vmem((CHUNKS, 16, 16, 128), bf16),
-                vmem((CHUNKS // 2, 16, 16, 128), bf16),
-                vmem((CHUNKS // 2, 8, 16, 128), bf16),
-                vmem((CHUNKS // 2, 8, 16, 128), bf16),
-                vmem((CHUNKS // 2, 8, 16, 128), bf16),
+                vmem((len(STRAIGHT), 16, 16, 128), bf16),
+                vmem((len(PAIRED), 8, 16, 128), bf16),
+                vmem((len(PAIRED), 8, 16, 128), bf16),
+                vmem((len(PAIRED), 8, 16, 128), bf16),
                 vmem((16, 128), f32),
                 vmem((4, PAD), f32),
                 pltpu.SemaphoreType.DMA((4 + CHUNKS,)),
-                pltpu.SemaphoreType.DMA((6 + CHUNKS + CHUNKS // 2,)),
-                pltpu.SemaphoreType.DMA((6 + CHUNKS + CHUNKS // 2,)),
+                pltpu.SemaphoreType.DMA((7 + CHUNKS + len(PAIRED),)),
+                pltpu.SemaphoreType.DMA((7 + CHUNKS + len(PAIRED),)),
             ],
             compiler_params=pltpu.CompilerParams(
                 collective_id=0, has_side_effects=True, vmem_limit_bytes=40 << 20

time: 61.8 us -> 60.4 us (0.977)
  Pallas kernels: 61 us -> 59.6 us
    pallas_call x1, Pallas kernels: 60.3 us -> 58.9 us  [shards(): pl.pallas_call(kernel, out_shape=tuple((jax.ShapeDtypeStruct(like.shape,...]
where the time goes in v3:
time: 60.4 us; the launch traced here: 60.2 us
  Pallas kernels  59.6 us (99%)
  between operations  0.64 us (1%)
    pallas_call x1, Pallas kernels, shards(): pl.pallas_call(kernel, out_shape=tuple((jax.ShapeDtypeStruct(like.shape,...  58.9 us

profile of v3, /device:TPU:1, one launch (start us, length us, event | category | flops | bytes accessed | tf_op | source)
XLA Modules:
  0.0 60.2 jit_solution(1037857597332263843)
XLA Ops:
  0.6 58.9 %shard_map.84 = (f32[1,256]{1,0:T(1,128)S(1)}, f32[1,256]{1,0:T(1,128)S(1)}, f32[4,2004]{1,0:T(4,128)S(1)}, f32[4,2004]{1,0:T(4,128)S(1)}) custom-call(s32[2004,256]{1,0:T(8,128)} %bitcast.1, f32[1,256]{1,0:T(1,128)} %u_factor.1, f32[1,256]{1,0:T(1,128)} %u_accum.1, f32[4,2004]{1,0:T(4,128)} %v_factor.1, f32[4,2004]{1,0:T(4,128)} %v_accum.1), custom_call_target="tpu_custom_call" | custom-call | tf_op jit(solution)/shard_map/pallas_call | solution.py:350
  59.5 0.7 %shard_map.85 = (f32[1,256]{1,0:T(1,128)}, f32[1,256]{1,0:T(1,128)}, f32[4,2004]{1,0:T(4,128)}, f32[4,2004]{1,0:T(4,128)}) custom-call(f32[1,256]{1,0:T(1,128)S(1)} %get-tuple-element.8.refs_0_, f32[1,256]{1,0:T(1,128)S(1)} %get-tuple-element.9.refs_1_, f32[4,2004]{1,0:T(4,128)S(1)} %get-tuple-element.10.refs_2_, f32[4,2004]{1,0:T(4,128)S(1)} %get-tuple-element.11.refs_3_), custom_call_target="tpu_custom_call" | custom-call | tf_op jit(solution)/shard_map/pallas_call | solution.py:396

commit v4 on v3

--- a/solution.py
+++ b/solution.py
@@ -13,7 +13,7 @@
 PAD = 2048
 CHUNK = 512
 CHUNKS = PAD // CHUNK
-PAIRED = (0, 1)
+PAIRED = (0,)
 STRAIGHT = tuple(q for q in range(CHUNKS) if q not in PAIRED)
 f32, bf16 = jnp.float32, jnp.bfloat16
 
@@ -118,7 +118,7 @@
     u_next, u_accum_next, v_next, v_accum_next,
     cnt, weight, u_in, ua_in, v_in, va_in, v_rows, u_row, ua_row,
     v_all, v_ranks, v_half, order, u_all, ua_all,
-    gu_out, gu_in, gu_z, u_rows, u_pair, u_got, fresh, gv_out, gv_in, gv_x, gv_mid, gv_y, gv_sum, g_tile,
+    gu_out, gu_in, gu_z, u_rows, u_pair, u_got, fresh, framed, spread, gv_out, gv_in, gv_x, gv_mid, gv_y, gv_sum, g_tile,
     local_sem, send_sem, recv_sem,
 ):
     half, z, core, y, x = place()
@@ -197,6 +197,8 @@
     col_rank = (col & 32) + (col & 15) * 2 + ((col >> 4) & 1)
     same = (((row >> 2) & 3) == (col >> 6)) & (rank == col_rank)
     order[...] = jnp.where(same, 1.0, 0.0).astype(bf16)
+
+    framed[...] = jnp.zeros((448, TEN_DEV), bf16)
 
     weight[PAD - 48 :, :] = jnp.zeros((48, TEN_DEV), bf16)
     for q in range(CHUNKS):
@@ -267,13 +269,22 @@
         wait_bytes(fresh, recv_sem.at[5])
 
     low = fresh[...].reshape(RANK, TEN_DEV)
+    framed[192:256, :] = low
+    for b in range(4):
+        spread[b] = jnp.dot(
+            order[...], framed[192 - 64 * b : 448 - 64 * b, :], preferred_element_type=f32
+        ).astype(bf16)
     for q in range(CHUNKS):
-        part = lax.dot_general(
-            low, residual(low, q), (((1,), (1,)), ((), ())), preferred_element_type=f32
-        ).astype(bf16)
-        stacked = jnp.concatenate([part[:, 128 * b : 128 * b + 128] for b in range(4)], axis=0)
-        pieces = jnp.dot(order[...], stacked, preferred_element_type=f32).astype(bf16)
-        gv_out[q] = pieces.reshape(16, 16, 128)
+        resid = residual(low, q)
+        pieces = jnp.zeros((256, 128), f32)
+        for b in range(4):
+            pieces += lax.dot_general(
+                spread[b],
+                resid[128 * b : 128 * b + 128, :],
+                (((1,), (1,)), ((), ())),
+                preferred_element_type=f32,
+            )
+        gv_out[q] = pieces.reshape(16, 16, 128).astype(bf16)
         if q in PAIRED:
             other = gv_out.at[q, pl.ds((1 - x) * 8, 8)]
             send(other, gv_x.at[PAIRED.index(q)], sems, 7 + q, ten_at(y, 1 - x))
@@ -377,6 +388,8 @@
                 vmem((2, TEN_DEV), f32),
                 vmem((2, TEN_DEV), f32),
                 vmem((2, 32, TEN_DEV), bf16),
+                vmem((448, TEN_DEV), bf16),
+                vmem((4, 256, TEN_DEV), bf16),
                 vmem((CHUNKS, 16, 16, 128), bf16),
                 vmem((len(STRAIGHT), 16, 16, 128), bf16),
                 vmem((len(PAIRED), 8, 16, 128), bf16),

time: 60.4 us -> 60.8 us (level)
  no operation moved by 1% of the time
where the time goes in v4:
time: 60.8 us; the launch traced here: 60.7 us
  Pallas kernels  60 us (99%)
  between operations  0.64 us (1%)
    pallas_call x1, Pallas kernels, shards(): pl.pallas_call(kernel, out_shape=tuple((jax.ShapeDtypeStruct(like.shape,...  59.4 us

profile of v4, /device:TPU:1, one launch (start us, length us, event | category | flops | bytes accessed | tf_op | source)
XLA Modules:
  0.0 60.7 jit_solution(10005461529957834478)
XLA Ops:
  0.6 59.4 %shard_map.84 = (f32[1,256]{1,0:T(1,128)S(1)}, f32[1,256]{1,0:T(1,128)S(1)}, f32[4,2004]{1,0:T(4,128)S(1)}, f32[4,2004]{1,0:T(4,128)S(1)}) custom-call(s32[2004,256]{1,0:T(8,128)} %bitcast.1, f32[1,256]{1,0:T(1,128)} %u_factor.1, f32[1,256]{1,0:T(1,128)} %u_accum.1, f32[4,2004]{1,0:T(4,128)} %v_factor.1, f32[4,2004]{1,0:T(4,128)} %v_accum.1), custom_call_target="tpu_custom_call" | custom-call | tf_op jit(solution)/shard_map/pallas_call | solution.py:361
  60.0 0.7 %shard_map.85 = (f32[1,256]{1,0:T(1,128)}, f32[1,256]{1,0:T(1,128)}, f32[4,2004]{1,0:T(4,128)}, f32[4,2004]{1,0:T(4,128)}) custom-call(f32[1,256]{1,0:T(1,128)S(1)} %get-tuple-element.8.refs_0_, f32[1,256]{1,0:T(1,128)S(1)} %get-tuple-element.9.refs_1_, f32[4,2004]{1,0:T(4,128)S(1)} %get-tuple-element.10.refs_2_, f32[4,2004]{1,0:T(4,128)S(1)} %get-tuple-element.11.refs_3_), custom_call_target="tpu_custom_call" | custom-call | tf_op jit(solution)/shard_map/pallas_call | solution.py:409

commit v5 on v4

--- a/solution.py
+++ b/solution.py
@@ -13,7 +13,7 @@
 PAD = 2048
 CHUNK = 512
 CHUNKS = PAD // CHUNK
-PAIRED = (0,)
+PAIRED = (0, 1)
 STRAIGHT = tuple(q for q in range(CHUNKS) if q not in PAIRED)
 f32, bf16 = jnp.float32, jnp.bfloat16
 

time: 60.8 us -> 60.5 us (level)
  no operation moved by 1% of the time
where the time goes in v5:
time: 60.5 us; the launch traced here: 60.3 us
  Pallas kernels  59.7 us (99%)
  between operations  0.64 us (1%)
    pallas_call x1, Pallas kernels, shards(): pl.pallas_call(kernel, out_shape=tuple((jax.ShapeDtypeStruct(like.shape,...  59 us

profile of v5, /device:TPU:1, one launch (start us, length us, event | category | flops | bytes accessed | tf_op | source)
XLA Modules:
  0.0 60.3 jit_solution(4649966076753031778)
XLA Ops:
  0.6 59.0 %shard_map.84 = (f32[1,256]{1,0:T(1,128)S(1)}, f32[1,256]{1,0:T(1,128)S(1)}, f32[4,2004]{1,0:T(4,128)S(1)}, f32[4,2004]{1,0:T(4,128)S(1)}) custom-call(s32[2004,256]{1,0:T(8,128)} %bitcast.1, f32[1,256]{1,0:T(1,128)} %u_factor.1, f32[1,256]{1,0:T(1,128)} %u_accum.1, f32[4,2004]{1,0:T(4,128)} %v_factor.1, f32[4,2004]{1,0:T(4,128)} %v_accum.1), custom_call_target="tpu_custom_call" | custom-call | tf_op jit(solution)/shard_map/pallas_call | solution.py:361
  59.7 0.7 %shard_map.85 = (f32[1,256]{1,0:T(1,128)}, f32[1,256]{1,0:T(1,128)}, f32[4,2004]{1,0:T(4,128)}, f32[4,2004]{1,0:T(4,128)}) custom-call(f32[1,256]{1,0:T(1,128)S(1)} %get-tuple-element.8.refs_0_, f32[1,256]{1,0:T(1,128)S(1)} %get-tuple-element.9.refs_1_, f32[4,2004]{1,0:T(4,128)S(1)} %get-tuple-element.10.refs_2_, f32[4,2004]{1,0:T(4,128)S(1)} %get-tuple-element.11.refs_3_), custom_call_target="tpu_custom_call" | custom-call | tf_op jit(solution)/shard_map/pallas_call | solution.py:409
